TPU v7x, 256 devices: a whole 4x4x8 slice. The times are simulated.
256 devices in a mesh: seq: 16 (over x_hi, z), tensor: 16 (over x_lo, y, core).
Axes of the slice: x: 4 (x_hi: 2, x_lo: 2; x = x_hi * 2 + x_lo), y: 4, z: 8, core: 2. Of those that a mesh axis runs over, the one named last changes fastest.
Arguments:
- attn_heads: bfloat16 [8192, 8192], P('seq', 'tensor'), may hold values from -6 to 6
- out_weight: bfloat16 [8192, 8192], P('tensor'), may hold values from -0.0625 to 0.0625
- residual: bfloat16 [8192, 8192], P('seq', 'tensor'), may hold values from -40 to 40
- norm_gain: bfloat16 [8192], P('tensor'), may hold values from 0.25 to 1.75
- proj: bfloat16 [8192, 4096], P('tensor', 'seq'), may hold values from -0.0625 to 0.0625
- student_hidden: bfloat16 [8192, 4096], P(('seq', 'tensor')), may hold values from -6 to 6
Outputs:
- mismatch: float32 [8192, 4096], P(('seq', 'tensor'))
- grad_proj: float32 [4096, 8192], P('seq', 'tensor')
All inputs are finite; a program needn't handle non-finite values.
Results may differ from a plain program's by a relative error of at most 0.015.
Values may be sent and summed in bfloat16 or wider, within the bound.
A program may use at most 128 MiB of HBM per device.

v0:
```python
import math

import jax
import jax.numpy as jnp
from jax import lax
from jax.sharding import PartitionSpec as P


def shards(attn_heads, out_weight, residual, norm_gain, proj, student_hidden):
    partial_sum = jnp.dot(attn_heads, out_weight, preferred_element_type=jnp.float32)
    summed = lax.psum_scatter(
        partial_sum.astype(jnp.bfloat16), "tensor", scatter_dimension=1, tiled=True
    ).astype(jnp.float32)
    hidden = residual.astype(jnp.float32) + summed
    power = lax.psum(jnp.sum(hidden * hidden, axis=1, keepdims=True), "tensor")
    full_width = hidden.shape[1] * lax.axis_size("tensor")
    normed = (
        hidden * lax.rsqrt(power / full_width + 1e-05) * norm_gain.astype(jnp.float32)
    ).astype(jnp.bfloat16)
    terms = jnp.dot(
        normed, lax.all_gather(proj, "seq", axis=1, tiled=True), preferred_element_type=jnp.float32
    )
    summed_rows = lax.psum_scatter(terms, "tensor", scatter_dimension=0, tiled=True)
    mismatch = summed_rows - student_hidden.astype(jnp.float32)
    full_rows = lax.all_gather(mismatch.astype(jnp.bfloat16), "tensor", axis=0, tiled=True)
    all_tokens = normed.shape[0] * lax.axis_size("seq")
    scale = 1.0 / math.sqrt(all_tokens)
    grad_proj = lax.psum_scatter(
        scale
        * lax.dot_general(
            full_rows, normed, (((0,), (0,)), ((), ())), preferred_element_type=jnp.float32
        ),
        "seq",
        scatter_dimension=0,
        tiled=True,
    )
    return (mismatch, grad_proj)


def solution(mesh):
    return jax.shard_map(
        shards,
        mesh=mesh,
        in_specs=(
            P("seq", "tensor"),
            P("tensor", None),
            P("seq", "tensor"),
            P("tensor"),
            P("tensor", "seq"),
            P(("seq", "tensor"), None),
        ),
        out_specs=(P(("seq", "tensor"), None), P("seq", "tensor")),
        check_vma=False,
    )
```

profile of v0, /device:TPU:8, one launch (start us, length us, event | category | flops | bytes accessed | tf_op | source)
XLA Modules:
  0.0 516.1 jit_solution(6913389379117711822)
XLA Ops:
  8.0 0.0 copy-start
  8.0 0.0 reduce-scatter.4.cloned.1.call-start
  8.1 1.0 copy-done
  9.0 10.1 %convolution_convert_fusion = bf16[512,8192]{1,0:T(8,128)(2,1)} fusion(bf16[512,512]{1,0:T(8,128)(2,1)S(1)} %copy-done, bf16[512,8192]{1,0:T(8,128)(2,1)} %param.7), kind=kOutput, calls=%fused_computation | convolution fusion | flops 4299161600 | bytes 17301504 | tf_op jit(solution)/shard_map/dot_general | solution.py:10
  19.1 0.0 copy-start.4
  19.1 0.0 copy-start.1
  19.1 0.0 reduce-scatter.4.cloned.1.call-update
  19.1 0.0 all-gather.3.cloned.1.call-start
  19.2 0.5 all-gather.3.cloned.1.call-update
  19.7 0.0 reduce-scatter.6.cloned.1.call-start
  19.8 0.0 copy-done.4
  19.8 98.6 %reduce-scatter.4.cloned.1.call-done = bf16[512,512]{1,0:T(8,128)(2,1)} async-done(((bf16[512,8192]{1,0:T(8,128)(2,1)}), bf16[512,512]{1,0:T(8,128)(2,1)}) %reduce-scatter.4.cloned.1.call-update) | async-done | bytes 524304 | tf_op jit(solution)/shard_map/reduce_scatter | solution.py:11
  118.4 0.0 copy-done.1
  118.4 1.3 multiply_reduce_fusion
  119.6 28.5 %psum.7 = f32[512,1]{0,1:T(1,128)S(1)} all-reduce(f32[512,1]{0,1:T(1,128)S(1)} %bitcast.8), channel_id=1, replica_groups=mesh['seq'=16,'tensor'=16] {'tensor'}, use_global_device_ids=true, to_apply=%region_2.0 | all-reduce | flops 512 | bytes 4096 | tf_op jit(solution)/shard_map/psum | solution.py:15
  148.2 0.0 all-gather.3.cloned.1.call-done
  148.2 0.0 copy-start.3
  148.2 8.0 %fusion = f32[512,4096]{1,0:T(8,128)} fusion(bf16[512,4096]{1,0:T(8,128)(2,1)} %all-gather.3.cloned.1.call-done, bf16[512,512]{1,0:T(8,128)(2,1)} %reduce-scatter.4.cloned.1.call-done, bf16[512,512]{1,0:T(8,128)(2,1)S(1)} %copy-done.1, f32[512]{0:T(512)S(1)} %convert_element_type.24, f32[512]{0:T(512)S(1)} %bitcast.6), kind=kOutput, calls=%fused_computation.7 | convolution fusion | flops 2149056512 | bytes 13635584 | tf_op jit(solution)/shard_map/dot_general | solution.py:20
  156.2 0.0 copy-start.2
  156.2 0.0 reduce-scatter.6.cloned.1.call-update
  156.2 0.0 all-gather.5.cloned.1.call-start
  156.3 75.9 %reduce-scatter.6.cloned.1.call-done = f32[32,4096]{1,0:T(8,128)} async-done(((f32[512,4096]{1,0:T(8,128)}), f32[32,4096]{1,0:T(8,128)}) %reduce-scatter.6.cloned.1.call-update) | async-done | bytes 524304 | tf_op jit(solution)/shard_map/reduce_scatter | solution.py:23
  232.2 0.0 copy-done.3
  232.2 2.0 fusion.1
  234.2 0.0 all-gather.5.cloned.1.call-update
  234.2 0.0 reduce-scatter.8.cloned.1.call-start
  234.3 43.0 %all-gather.5.cloned.1.call-done = bf16[512,4096]{1,0:T(8,128)(2,1)} async-done(((bf16[32,4096]{1,0:T(8,128)(2,1)}), bf16[512,4096]{1,0:T(8,128)(2,1)}) %all-gather.5.cloned.1.call-update) | async-done | bytes 4194320 | tf_op jit(solution)/shard_map/all_gather | solution.py:25
  277.3 0.0 copy-done.2
  277.3 7.9 %convolution_multiply_fusion = f32[4096,512]{1,0:T(8,128)} fusion(bf16[512,4096]{1,0:T(8,128)(2,1)} %all-gather.5.cloned.1.call-done, bf16[512,512]{1,0:T(8,128)(2,1)S(1)} %copy-done.2, bf16[512,512]{1,0:T(8,128)(2,1)S(1)} %copy-done.1, f32[512]{0:T(512)S(1)} %convert_element_type.24, f32[512]{0:T(512)S(1)} %bitcast.7), kind=kOutput, calls=%fused_computation.1 | convolution fusion | flops 2151153664 | bytes 13635584 | tf_op jit(solution)/shard_map/dot_general | solution.py:30
  285.2 0.0 reduce-scatter.8.cloned.1.call-update
  285.2 223.8 %reduce-scatter.8.cloned.1.call-done = f32[256,512]{1,0:T(8,128)} async-done(((f32[4096,512]{1,0:T(8,128)}), f32[256,512]{1,0:T(8,128)}) %reduce-scatter.8.cloned.1.call-update) | async-done | bytes 524304 | tf_op jit(solution)/shard_map/reduce_scatter | solution.py:28
  (2 shorter events, 0.0 us)
Async XLA Ops:
  8.0 1.0 copy-start
  8.0 110.3 %reduce-scatter.4.cloned.1.call-start = ((), (), s32[]{:S(2)}) async-start(), calls=%async_computation.3 | async-start | bytes 8912896 | tf_op jit(solution)/shard_map/reduce_scatter | solution.py:11
  19.1 0.7 copy-start.4
  19.1 99.2 %copy-start.1 = (bf16[512,512]{1,0:T(8,128)(2,1)S(1)}, bf16[512,512]{1,0:T(8,128)(2,1)}, u32[]{:S(2)}) copy-start(bf16[512,512]{1,0:T(8,128)(2,1)} %param.8) | copy-start | bytes 1572868
  19.1 129.0 %all-gather.3.cloned.1.call-start = ((), (), s32[]{:S(2)}) async-start(), calls=%async_computation.4 | async-start | bytes 4456448 | tf_op jit(solution)/shard_map/all_gather | solution.py:21
  19.7 212.5 %reduce-scatter.6.cloned.1.call-start = ((), (), s32[]{:S(2)}) async-start(), calls=%async_computation.5 | async-start | bytes 8912896 | tf_op jit(solution)/shard_map/reduce_scatter | solution.py:23
  148.2 84.0 %copy-start.3 = (bf16[32,4096]{1,0:T(8,128)(2,1)S(1)}, bf16[32,4096]{1,0:T(8,128)(2,1)}, u32[]{:S(2)}) copy-start(bf16[32,4096]{1,0:T(8,128)(2,1)} %param.11) | copy-start | bytes 786436
  156.2 121.1 %copy-start.2 = (bf16[512,512]{1,0:T(8,128)(2,1)S(1)}, bf16[512,512]{1,0:T(8,128)(2,1)}, u32[]{:S(2)}) copy-start(bf16[512,512]{1,0:T(8,128)(2,1)} %reduce-scatter.4.cloned.1.call-done) | copy-start | bytes 1572868
  156.2 121.1 %all-gather.5.cloned.1.call-start = ((), (), s32[]{:S(2)}) async-start(), calls=%async_computation.6 | async-start | bytes 4456448 | tf_op jit(solution)/shard_map/all_gather | solution.py:25
  234.2 274.8 %reduce-scatter.8.cloned.1.call-start = ((), (), s32[]{:S(2)}) async-start(), calls=%async_computation.7 | async-start | bytes 8912896 | tf_op jit(solution)/shard_map/reduce_scatter | solution.py:28
Sparse Core Ops, SparseCore 0:
  19.3 99.0 reduce-scatter.3
  156.4 75.8 reduce-scatter.5
  234.6 42.6 all-gather.4
Sparse Core Ops, SparseCore 1:
  22.1 108.8 all-gather.2
  285.3 223.6 reduce-scatter.7
where the time goes:
time: 516 us
  waiting for transfers between devices  442 us (86%)
  blocking collectives  28.5 us (6%)
  matrix products  26 us (5%)
  between operations  15.2 us (3%)
    reduce_scatter x1, waiting for transfers between devices, shards(): lax.psum_scatter(scale * lax.dot_general(full_rows, normed, (((0,), (0,))...  224 us
    reduce_scatter x1, waiting for transfers between devices, shards(): lax.psum_scatter(partial_sum.astype(jnp.bfloat16), 'tensor', scatter_dime...  98.6 us
    reduce_scatter x1, waiting for transfers between devices, shards(): lax.psum_scatter(terms, 'tensor', scatter_dimension=0, tiled=True)  75.9 us
    all_gather x1, waiting for transfers between devices, shards(): lax.all_gather(mismatch.astype(jnp.bfloat16), 'tensor', axis=0, tiled=True)  43 us
    psum x1, blocking collectives, shards(): power = lax.psum(jnp.sum(hidden * hidden, axis=1, keepdims=True), 'tensor')  28.5 us
  transfers between devices with their start and end apart: 5, of which 4 were waited for; matrix products, arithmetic and copies ran while one was open for 0% of the time, Pallas kernels for 0%

commit v1 on v0

v1 whole, which is shorter than its diff:
```python
import math

import jax
import jax.numpy as jnp
from jax import lax
from jax.experimental import pallas as pl
from jax.experimental.pallas import tpu as pltpu
from jax.sharding import PartitionSpec as P

MESH = pl.DeviceIdType.MESH
F32 = jnp.float32
BF16 = jnp.bfloat16
PAIRS = 8
STAGES = 7


def dot(a, b, dims=((1,), (0,))):
    return lax.dot_general(a, b, (dims, ((), ())), preferred_element_type=F32)


def kernel(
    attn, weight, resid, gain, proj, student,
    mis_out, grad_out,
    attn_v, res_v, w_v, stu_v,
    a_send, a_own, a_crecv, a_xrecv, ya_half, ya_full, yb_half, yb_full, xb_recv,
    hg, pw, pw_recv, r_v,
    pj,
    t_send, t_own, t_crecv, xr0, yr0, yr1, xr1, m_all,
    g_send, ring, rx,
    sem_attn, sem_res, sem_stu, sem_w, sem_proj,
    ac_s, ac_r, ax_s, ax_r, ay_s, ay_r, by_s, by_r, bx_s, bx_r,
    pw_s, pw_r, cx_s, cx_r, cz_s, cz_r,
    d_s, d_r, f_s, f_r, fx_s, fx_r,
):
    s = lax.axis_index("seq")
    t = lax.axis_index("tensor")
    xh, z = s // 8, s % 8
    x, y, c = t // 8, (t // 2) % 4, t % 2

    def at(xh_, z_, x_, y_, c_):
        return (xh_ * 8 + z_, x_ * 8 + y_ * 2 + c_)

    sib = at(xh, z, x, y, 1 - c)
    xdev = at(xh, z, 1 - x, y, c)
    xhdev = at(1 - xh, z, x, y, c)
    zdev = (at(xh, (z + 1) % 8, x, y, c), at(xh, (z + 7) % 8, x, y, c))

    def ydev(o):
        return at(xh, z, x, (y + o) % 4, c)

    def remote(src, dst, ss, rs, dev):
        return pltpu.make_async_remote_copy(
            src_ref=src, dst_ref=dst, send_sem=ss, recv_sem=rs, device_id=dev, device_id_type=MESH
        )

    def tokens(i):
        return (i % 8) // 4 * 8 + (i % 4) * 2 + i // 8

    def load_rows(src, dst, sem):
        def one(i, carry):
            row = pl.multiple_of(tokens(i) * 32, 32)
            pltpu.make_async_copy(src.at[pl.ds(row, 32)], dst.at[i], sem).start()
            return carry

        lax.fori_loop(0, 16, one, 0)

    def block_of(j, xo, co):
        dy = 2 - j + (j // 2) * (3 - 2 * (j % 2))
        return xo * 8 + (y + dy) % 4 * 2 + co

    def load_w(j):
        def one(i, carry):
            b = block_of(j, (x + 1 + i % 2) % 2, (c + 1 + i // 2) % 2)
            col = pl.multiple_of(b * 512, 512)
            pltpu.make_async_copy(weight.at[:, pl.ds(col, 512)], w_v.at[b], sem_w.at[b]).start()
            return carry

        lax.fori_loop(0, 4, one, 0)

    pltpu.make_async_copy(proj, pj.at[s], sem_proj).start()
    load_rows(attn, attn_v, sem_attn)
    for j in range(4):
        load_w(j)
    load_rows(resid, res_v, sem_res)
    pltpu.make_async_copy(student, stu_v, sem_stu).start()

    ring[:, 0, 0, 128:256] = jnp.zeros((2, 128, 512), BF16)
    ring[:, 1, 0, 0:128] = jnp.zeros((2, 128, 512), BF16)

    barrier = pltpu.get_barrier_semaphore()

    def greet(i, carry):
        pl.semaphore_signal(barrier, inc=1, device_id=(s, (t + i) % 16), device_id_type=MESH)
        return carry

    lax.fori_loop(1, 16, greet, 0)
    for dev in (xhdev,) + zdev:
        pl.semaphore_signal(barrier, inc=1, device_id=dev, device_id_type=MESH)
    pl.semaphore_wait(barrier, 18)

    def cz(line, dr, j):
        sign = 1 - 2 * dr
        xx = xh if line == 1 else 1 - xh
        b = xx * 8 + (z - sign * (j - 1) + 8) % 8
        ref = pj.at[b]
        if j == 4:
            ref = pj.at[b, pl.ds(256 * dr, 256)]
        return remote(ref, ref, cz_s.at[line, dr, j - 1], cz_r.at[line, dr, j - 1], zdev[dr])

    def cx():
        return remote(pj.at[s], pj.at[s], cx_s, cx_r, xhdev)

    def forward(line, j):
        for dr in range(2):
            if j > 1:
                cz(line, dr, j - 1).wait_recv()
            cz(line, dr, j).start()

    pltpu.make_async_copy(proj, pj.at[s], sem_proj).wait()
    cx().start()
    forward(1, 1)

    def ac(j, xo):
        return remote(a_send.at[j, xo], a_crecv.at[j, xo], ac_s.at[j, xo], ac_r.at[j, xo], sib)

    def ax(j):
        return remote(a_own.at[j, 1 - x, pl.ds(0, 256)], a_xrecv.at[j], ax_s.at[j], ax_r.at[j], xdev)

    def a_half(dr):
        return remote(
            a_own.at[0, x, pl.ds(128 * dr, 128)], ya_half.at[dr], ay_s.at[0, dr], ay_r.at[0, dr], ydev(1 + 2 * dr)
        )

    def a_full(dr):
        return remote(
            a_own.at[1 + dr, x, pl.ds(0, 256)], ya_full.at[dr], ay_s.at[1, dr], ay_r.at[1, dr], ydev(1 + 2 * dr)
        )

    def b_half(dr):
        return remote(
            a_own.at[0, :, pl.ds(256 + 128 * dr, 128)], yb_half.at[dr], by_s.at[0, dr], by_r.at[0, dr],
            ydev(1 + 2 * dr),
        )

    def b_full(dr):
        return remote(
            a_own.at[1 + dr, :, pl.ds(256, 256)], yb_full.at[dr], by_s.at[1, dr], by_r.at[1, dr], ydev(1 + 2 * dr)
        )

    def bx():
        return remote(a_own.at[3, 1 - x, pl.ds(256, 256)], xb_recv, bx_s, bx_r, xdev)

    def product(j, xo, co, out):
        b = block_of(j, xo, co)
        col = pl.multiple_of(b * 512, 512)
        pltpu.make_async_copy(weight.at[:, pl.ds(col, 512)], w_v.at[b], sem_w.at[b]).wait()
        out[j, xo] = dot(attn_v[...].reshape(512, 512), w_v[b]).astype(BF16)

    def multiply(j):
        def other(i, carry):
            xo = (x + 1 + i) % 2
            product(j, xo, 1 - c, a_send)
            ac(j, xo).start()
            return carry

        def own(i, carry):
            product(j, (x + 1 + i) % 2, c, a_own)
            return carry

        lax.fori_loop(0, 2, other, 0)
        lax.fori_loop(0, 2, own, 0)

    def combine(j):
        def one(i, carry):
            xo = (x + 1 + i) % 2
            ac(j, xo).wait_recv()
            a_own[j, xo] = (a_own[j, xo].astype(F32) + a_crecv[j, xo].astype(F32)).astype(BF16)

            @pl.when(i == 0)
            def _():
                ax(j).start()

            return carry

        lax.fori_loop(0, 2, one, 0)

        @pl.when(j == 0)
        def _():
            b_half(0).start()
            b_half(1).start()

    pltpu.make_async_copy(attn, attn, sem_attn).wait()

    def teacher(i, carry):
        @pl.when(i < 4)
        def _():
            multiply(i)

        @pl.when(i >= 1)
        def _():
            combine(i - 1)

        return carry

    lax.fori_loop(0, 5, teacher, 0)
    cx().wait_recv()
    forward(0, 1)
    forward(1, 2)

    def add_a(j):
        ax(j).wait_recv()
        a_own[j, x, 0:256] = (a_own[j, x, 0:256].astype(F32) + a_xrecv[j].astype(F32)).astype(BF16)

    add_a(0)
    for dr in range(2):
        a_half(dr).start()
    for dr in range(2):
        rows = slice(256 + 128 * dr, 384 + 128 * dr)
        b_half(dr).wait_recv()
        a_own[1 + dr, :, rows] = (a_own[1 + dr, :, rows].astype(F32) + yb_half[dr].astype(F32)).astype(BF16)
        b_full(dr).start()
    forward(0, 2)
    forward(1, 3)
    for dr in range(2):
        rows = slice(128 * dr, 128 * dr + 128)
        add_a(1 + dr)
        a_half(dr).wait_recv()
        a_own[1 + dr, x, rows] = (a_own[1 + dr, x, rows].astype(F32) + ya_half[dr].astype(F32)).astype(BF16)
        a_full(dr).start()
    b_full(0).wait_recv()
    b_full(1).wait_recv()
    a_own[3, :, 256:512] = (
        a_own[3, :, 256:512].astype(F32) + yb_full[0].astype(F32) + yb_full[1].astype(F32)
    ).astype(BF16)
    bx().start()
    forward(0, 3)
    add_a(3)
    a_full(0).wait_recv()
    a_full(1).wait_recv()
    pltpu.make_async_copy(resid, resid, sem_res).wait()

    def finish(co, total):
        hidden = total + res_v[pl.ds(8 * co, 8)].astype(F32).reshape(256, 512)
        hg[co] = (hidden * gain[...].astype(F32)).astype(BF16)
        sq = hidden * hidden
        sq = sq[:, 0:128] + sq[:, 128:256] + sq[:, 256:384] + sq[:, 384:512]
        pw[pl.ds(8 * co, 8)] = sq.reshape(8, 32, 128)

    finish(0, a_own[3, x, 0:256].astype(F32) + ya_full[0].astype(F32) + ya_full[1].astype(F32))
    forward(1, 4)
    bx().wait_recv()
    finish(1, a_own[3, x, 256:512].astype(F32) + xb_recv[...].astype(F32))

    def power(i):
        to = (t + i) % 16
        return remote(
            pw.at[to % 2 * 8 + to // 8 * 4 + to // 2 % 4], pw_recv.at[i], pw_s.at[i], pw_r.at[i], (s, to)
        )

    def send_power(i, carry):
        power(i).start()
        return carry

    lax.fori_loop(1, 16, send_power, 0)
    forward(0, 4)

    def root():
        def one(i, total):
            power(i).wait_recv()
            power(i).wait_send()
            return total + pw_recv[i]

        total = lax.fori_loop(1, 16, one, pw[c * 8 + x * 4 + y])
        mean = jnp.sum(total, axis=1, keepdims=True) * (1.0 / 8192)
        r_v[...] = jnp.broadcast_to(lax.rsqrt(mean + 1e-05), (32, 256))

    pltpu.make_async_copy(student, stu_v, sem_stu).wait()
    for line in range(2):
        for dr in range(2):
            cz(line, dr, 4).wait_recv()

    def block(g, m):
        mid = 1 - (g + 1) // 8 - (7 - g) // 7
        line = (1 - mid) * m + mid * ((g + 1) % 2)
        xx = (xh + 1 + line) % 2
        off = (1 - 2 * m) * (4 - (g + 1) // 2)
        return xx * 8 + (z + off + 8) % 8

    def ds_(k, i):
        return d_s.at[k, i], d_r.at[k, i]

    def dc(k):
        return remote(t_send.at[k], t_crecv.at[k], *ds_(k, 0), sib)

    def dx(g, m):
        k = 2 * g + m
        if m == 0:
            return remote(t_own.at[k, 1 - x], xr0.at[g], *ds_(k, 1), xdev)
        return remote(t_own.at[k, 1 - x, y], xr1.at[g], *ds_(k, 1), xdev)

    def dy(g, m, o):
        k = 2 * g + m
        if m == 0:
            return remote(t_own.at[k, x, (y + o) % 4], yr0.at[g, o - 1], *ds_(k, 1 + o), ydev(o))
        return remote(t_own.at[k, :, (y + o) % 4], yr1.at[g, o - 1], *ds_(k, 1 + o), ydev(o))

    def ex(g, m):
        k = 2 * g + m
        ref = m_all.at[k, c, x] if m == 0 else m_all.at[k, c, x, y]
        return remote(ref, ref, *ds_(k, 5), xdev)

    def ey(g, m, o):
        k = 2 * g + m
        ref = m_all.at[k, c, x, y] if m == 0 else m_all.at[k, c, :, y]
        return remote(ref, ref, *ds_(k, 5 + o), ydev(o))

    def ec(k):
        return remote(m_all.at[k, c], m_all.at[k, c], *ds_(k, 9), sib)

    def fz(line, dr, j, src):
        dst = ring.at[line, dr, j]
        return remote(src, dst, f_s.at[line, dr, j], f_r.at[line, dr, j], zdev[dr])

    def fz_half(line, dr):
        rows = pl.ds(128 * dr, 128)
        return remote(
            g_send.at[line, rows], ring.at[line, dr, 0, rows], f_s.at[line, dr, 0], f_r.at[line, dr, 0], zdev[dr]
        )

    def fx():
        return remote(g_send.at[14], rx, fx_s, fx_r, xhdev)

    def stage0(g, m):
        k = 2 * g + m
        b = block(g, m)
        t_send[k] = dot(hg[1 - c], pj[b]).astype(BF16).reshape(2, 4, 32, 256)
        dc(k).start()
        t_own[k] = dot(hg[c], pj[b]).astype(BF16).reshape(2, 4, 32, 256)

    def stage1(g, m):
        k = 2 * g + m
        dc(k).wait_recv()
        t_own[k] = (t_own[k].astype(F32) + t_crecv[k].astype(F32)).astype(BF16)
        if m == 0:
            dx(g, m).start()
        else:
            for o in (2, 1, 3):
                dy(g, m, o).start()

    def stage2(g, m):
        k = 2 * g + m
        dc(k).wait_send()
        if m == 0:
            dx(g, m).wait_recv()
            t_own[k, x] = (t_own[k, x].astype(F32) + xr0[g].astype(F32)).astype(BF16)
            for o in (2, 1, 3):
                dy(g, m, o).start()
        else:
            total = t_own[k, :, y].astype(F32)
            for o in (1, 2, 3):
                dy(g, m, o).wait_recv()
                total = total + yr1[g, o - 1].astype(F32)
            t_own[k, :, y] = total.astype(BF16)
            dx(g, m).start()

    def stage3(g, m):
        k = 2 * g + m
        if m == 0:
            total = t_own[k, x, y].astype(F32)
            for o in (1, 2, 3):
                dy(g, m, o).wait_recv()
                total = total + yr0[g, o - 1].astype(F32)
        else:
            dx(g, m).wait_recv()
            total = t_own[k, x, y].astype(F32) + xr1[g].astype(F32)
        cols = pl.ds(pl.multiple_of(block(g, m) * 256, 256), 256)
        mismatch = total * r_v[...] - stu_v[:, cols].astype(F32)
        mis_out[:, cols] = mismatch
        m_all[k, c, x, y] = (mismatch * r_v[...]).astype(BF16)
        if m == 0:
            for o in (2, 1, 3):
                ey(g, m, o).start()
        else:
            ex(g, m).start()
        dx(g, m).wait_send()
        for o in (1, 2, 3):
            dy(g, m, o).wait_send()

    def stage4(g, m):
        if m == 0:
            for o in (1, 2, 3):
                ey(g, m, o).wait_recv()
            ex(g, m).start()
        else:
            ex(g, m).wait_recv()
            for o in (2, 1, 3):
                ey(g, m, o).start()

    def stage5(g, m):
        if m == 0:
            ex(g, m).wait_recv()
        else:
            for o in (1, 2, 3):
                ey(g, m, o).wait_recv()
        ec(2 * g + m).start()
        ex(g, m).wait_send()
        for o in (1, 2, 3):
            ey(g, m, o).wait_send()

    def stage6(g, m):
        k = 2 * g + m
        ec(k).wait_recv()
        part = dot(m_all[k].reshape(512, 256), hg[...].reshape(512, 512), ((0,), (0,)))

        @pl.when(g == 0)
        def _():
            g_send[m] = part.astype(BF16)
            fz_half(m, 0).start()
            fz_half(m, 1).start()

        @pl.when((g > 0) & (g < 7))
        def _():
            line, j = (g + 1) % 2, (g + 1) // 2 - 1

            @pl.when(j == 0)
            def _():
                fz_half(line, m).wait_recv()

            @pl.when(j > 0)
            def _():
                fz(line, m, j, g_send.at[k]).wait_recv()

            g_send[k] = (part + ring[line, m, j].astype(F32)).astype(BF16)
            fz(line, m, j + 1, g_send.at[k]).start()

        @pl.when(g == 7)
        def _():
            fz(m, 0, 3, g_send.at[k]).wait_recv()
            fz(m, 1, 3, g_send.at[k]).wait_recv()
            total = part + ring[m, 0, 3].astype(F32) + ring[m, 1, 3].astype(F32)
            if m == 0:
                g_send[k] = total.astype(BF16)
                fx().start()
            else:
                fx().wait_recv()
                grad_out[...] = (total + rx[...].astype(F32)) * (1.0 / math.sqrt(8192))

        ec(k).wait_send()

    stages = (stage0, stage1, stage2, stage3, stage4, stage5, stage6)

    def student_step(i, carry):
        for n in reversed(range(STAGES)):
            @pl.when((i >= n) & (i < PAIRS + n))
            def _():
                stages[n](i - n, 0)
                stages[n](i - n, 1)

        @pl.when(i == 2)
        def _():
            root()

        return carry

    lax.fori_loop(0, PAIRS + STAGES - 1, student_step, 0)

    cx().wait_send()
    for line in range(2):
        for dr in range(2):
            for j in range(1, 5):
                cz(line, dr, j).wait_send()
            fz_half(line, dr).wait_send()
            for j in range(1, 4):
                fz(line, dr, j, g_send.at[0]).wait_send()
    for j in range(4):
        for xo in range(2):
            ac(j, xo).wait_send()
        ax(j).wait_send()
    for dr in range(2):
        a_half(dr).wait_send()
        a_full(dr).wait_send()
        b_half(dr).wait_send()
        b_full(dr).wait_send()
    bx().wait_send()
    fx().wait_send()


def shards(attn_heads, out_weight, residual, norm_gain, proj, student_hidden):
    hbm = pl.BlockSpec(memory_space=pl.ANY)
    vmem = pl.BlockSpec(memory_space=pltpu.VMEM)
    buf = lambda *shape: pltpu.VMEM(shape, BF16)
    dma = lambda *shape: pltpu.SemaphoreType.DMA(shape)
    return pl.pallas_call(
        kernel,
        name="distill",
        out_shape=(
            jax.ShapeDtypeStruct((32, 4096), F32),
            jax.ShapeDtypeStruct((256, 512), F32),
        ),
        in_specs=[hbm, hbm, hbm, vmem, hbm, hbm],
        out_specs=(vmem, vmem),
        scratch_shapes=[
            buf(16, 32, 512), buf(16, 32, 512), buf(16, 512, 512), buf(32, 4096),
            buf(4, 2, 512, 512), buf(4, 2, 512, 512), buf(4, 2, 512, 512), buf(4, 256, 512),
            buf(2, 128, 512), buf(2, 256, 512), buf(2, 2, 128, 512), buf(2, 2, 256, 512), buf(256, 512),
            buf(2, 256, 512), pltpu.VMEM((16, 32, 128), F32), pltpu.VMEM((16, 32, 128), F32),
            pltpu.VMEM((32, 256), F32),
            buf(16, 512, 256),
            buf(16, 2, 4, 32, 256), buf(16, 2, 4, 32, 256), buf(16, 2, 4, 32, 256),
            buf(8, 4, 32, 256), buf(8, 3, 32, 256), buf(8, 3, 2, 32, 256), buf(8, 32, 256),
            buf(16, 2, 2, 4, 32, 256),
            buf(16, 256, 512), buf(2, 2, 4, 256, 512), buf(256, 512),
            dma(), dma(), dma(), dma(16), dma(),
            dma(4, 2), dma(4, 2), dma(4), dma(4), dma(2, 2), dma(2, 2), dma(2, 2), dma(2, 2), dma(), dma(),
            dma(16), dma(16), dma(), dma(), dma(2, 2, 4), dma(2, 2, 4),
            dma(16, 10), dma(16, 10), dma(2, 2, 4), dma(2, 2, 4), dma(), dma(),
        ],
        compiler_params=pltpu.CompilerParams(
            collective_id=0, has_side_effects=True, vmem_limit_bytes=62 * 2**20
        ),
    )(attn_heads, out_weight, residual, norm_gain.reshape(1, 512), proj, student_hidden)


def solution(mesh):
    return jax.shard_map(
        shards,
        mesh=mesh,
        in_specs=(
            P("seq", "tensor"),
            P("tensor", None),
            P("seq", "tensor"),
            P("tensor"),
            P("tensor", "seq"),
            P(("seq", "tensor"), None),
        ),
        out_specs=(P(("seq", "tensor"), None), P("seq", "tensor")),
        check_vma=False,
    )
```

time: 516 us -> 130 us (0.25)
  waiting for transfers between devices: 442 us -> 0 us
  Pallas kernels: 0 us -> 124 us
  blocking collectives: 28.5 us -> 0 us
  matrix products: 26 us -> 0 us
  between operations: 15.2 us -> 0.64 us
    reduce_scatter x3 -> x0, waiting for transfers between devices: 398 us -> none  [the longest x1 224 us: shards(): lax.psum_scatter(scale * lax.dot_general(full_rows, normed, (((0,), (0,))...]
    pallas_call x0 -> x1, Pallas kernels: none -> 124 us  [shards(): pl.pallas_call(kernel, name='distill', out_shape=(jax.ShapeDtypeStruct((3...]
    all_gather x2 -> x0, waiting for transfers between devices: 43 us -> none  [the longest x1 43 us: shards(): lax.all_gather(mismatch.astype(jnp.bfloat16), 'tensor', axis=0, tiled=True)]
    psum x1 -> x0, blocking collectives: 28.5 us -> none  [shards(): power = lax.psum(jnp.sum(hidden * hidden, axis=1, keepdims=True), 'tensor')]
    dot_general x3 -> x0, matrix products: 26 us -> none  [the longest x1 10.1 us: shards(): jnp.dot(attn_heads, out_weight, preferred_element_type=jnp.float32)]
  transfers between devices with their start and end apart: 5 -> 0, of which waited for: 4 -> 0; matrix products, arithmetic and copies ran while one was open for 0% -> 0% of each run, Pallas kernels for 0% -> 0%
where the time goes in v1:
time: 130 us
  Pallas kernels  124 us (95%)
  local copies, waits for them, and re-layouts  5 us (4%)
    pallas_call x1, Pallas kernels, shards(): pl.pallas_call(kernel, name='distill', out_shape=(jax.ShapeDtypeStruct((3...  124 us
    unnamed x2, local copies, waits for them, and re-layouts  3.74 us

profile of v1, /device:TPU:8, one launch (start us, length us, event | category | flops | bytes accessed | tf_op | source)
XLA Modules:
  0.0 129.5 jit_solution(10484705031815427602)
XLA Ops:
  0.6 1.3 reshape.7.gain
  1.9 123.9 %distill.1 = (f32[32,4096]{1,0:T(8,128)}, f32[256,512]{1,0:T(8,128)}) custom-call(bf16[512,512]{1,0:T(8,128)(2,1)} %attn.1, bf16[512,8192]{1,0:T(8,128)(2,1)} %weight.1, bf16[512,512]{1,0:T(8,128)(2,1)} %resid.1, bf16[1,512]{1,0:T(2,128)(2,1)} %reshape.7.gain, bf16[512,256]{1,0:T(8,128)(2,1)} %proj.1, bf16[32,4096]{1,0:T(8,128)(2,1)} %student.1), custom_call_target="tpu_custom_call" | custom-call | tf_op jit(solution)/shard_map/distill/pallas_call | solution.py:493
  125.8 1.9 %copy.10 = f32[32,4096]{1,0:T(8,128)} copy(f32[32,4096]{1,0:T(8,128)} %get-tuple-element.4) | data formatting | bytes 1048576
  127.7 1.9 %copy.11 = f32[256,512]{1,0:T(8,128)} copy(f32[256,512]{1,0:T(8,128)} %get-tuple-element.5) | data formatting | bytes 1048576

commit v2 on v1

v2 whole, which is shorter than its diff:
```python
import math

import jax
import jax.numpy as jnp
from jax import lax
from jax.experimental import pallas as pl
from jax.experimental.pallas import tpu as pltpu
from jax.sharding import PartitionSpec as P

MESH = pl.DeviceIdType.MESH
F32 = jnp.float32
BF16 = jnp.bfloat16
BLOCKS = 8
STEPS = (0, 1, 3, 5, 7, 9, 10, 11)
ROWS_A = 160
HALF_A, HALF_B = ROWS_A // 2, (512 - ROWS_A) // 2


def dot(a, b, dims=((1,), (0,))):
    return lax.dot_general(a, b, (dims, ((), ())), preferred_element_type=F32)


def kernel(
    attn, weight, resid, gain, proj, student,
    mis_out, grad_out,
    attn_v, res_v, w_v, stu_v,
    a_send, a_own, a_crecv, a_xrecv, ya_half, ya_full, yb_half, yb_full, xb_recv,
    hg, pw, pw_recv, r_v,
    pj,
    t_send, t_own, t_crecv, xr0, yr0, yr1, xr1, m_all,
    g_acc, g_send, ring, rx, mis_v, grad_v,
    sem_attn, sem_res, sem_stu, sem_w, sem_proj, sem_mis, sem_grad,
    ac_s, ac_r, ax_s, ax_r, ay_s, ay_r, by_s, by_r, bx_s, bx_r,
    pw_s, pw_r, cx_s, cx_r, cz_s, cz_r,
    d_s, d_r, f_s, f_r, fx_s, fx_r,
):
    s = lax.axis_index("seq")
    t = lax.axis_index("tensor")
    xh, z = s // 8, s % 8
    x, y, c = t // 8, (t // 2) % 4, t % 2

    def at(xh_, z_, x_, y_, c_):
        return (xh_ * 8 + z_, x_ * 8 + y_ * 2 + c_)

    sib = at(xh, z, x, y, 1 - c)
    xdev = at(xh, z, 1 - x, y, c)
    xhdev = at(1 - xh, z, x, y, c)
    zdev = (at(xh, (z + 1) % 8, x, y, c), at(xh, (z + 7) % 8, x, y, c))

    def ydev(o):
        return at(xh, z, x, (y + o) % 4, c)

    def remote(src, dst, ss, rs, dev):
        return pltpu.make_async_remote_copy(
            src_ref=src, dst_ref=dst, send_sem=ss, recv_sem=rs, device_id=dev, device_id_type=MESH
        )

    barrier = pltpu.get_barrier_semaphore()

    def greet(i, carry):
        pl.semaphore_signal(barrier, inc=1, device_id=(s, (t + i) % 16), device_id_type=MESH)
        return carry

    lax.fori_loop(1, 16, greet, 0)
    for dev in (xhdev,) + zdev:
        pl.semaphore_signal(barrier, inc=1, device_id=dev, device_id_type=MESH)

    def tokens(i):
        return (i % 8) // 4 * 8 + (i % 4) * 2 + i // 8

    def load_rows(src, dst, sem):
        def one(i, carry):
            row = pl.multiple_of(tokens(i) * 32, 32)
            pltpu.make_async_copy(src.at[pl.ds(row, 32)], dst.at[i], sem).start()
            return carry

        lax.fori_loop(0, 16, one, 0)

    def block_of(j, xo, co):
        dy = 2 - j + (j // 2) * (3 - 2 * (j % 2))
        return xo * 8 + (y + dy) % 4 * 2 + co

    def load_w(j):
        def one(i, carry):
            b = block_of(j, (x + 1 + i % 2) % 2, (c + 1 + i // 2) % 2)
            col = pl.multiple_of(b * 512, 512)
            pltpu.make_async_copy(weight.at[:, pl.ds(col, 512)], w_v.at[b], sem_w.at[b]).start()
            return carry

        lax.fori_loop(0, 4, one, 0)

    pltpu.make_async_copy(proj, pj.at[s], sem_proj).start()
    load_rows(attn, attn_v, sem_attn)
    for j in range(4):
        load_w(j)
    load_rows(resid, res_v, sem_res)
    pltpu.make_async_copy(student, stu_v, sem_stu).start()

    ring[:, 0, 0, 128:256] = jnp.zeros((2, 128, 512), BF16)
    ring[:, 1, 0, 0:128] = jnp.zeros((2, 128, 512), BF16)

    pl.semaphore_wait(barrier, 18)

    def cz(line, dr, j, p):
        sign = 1 - 2 * dr
        xx = xh if line == 1 else 1 - xh
        b = xx * 8 + (z - sign * (j - 1) + 8) % 8
        if j == 4:
            ref = pj.at[b, pl.ds(256 * dr + 128 * p, 128)]
        else:
            ref = pj.at[b, pl.ds(256 * p, 256)]
        return remote(ref, ref, cz_s.at[line, dr, j - 1, p], cz_r.at[line, dr, j - 1, p], zdev[dr])

    def cx():
        return remote(pj.at[s], pj.at[s], cx_s, cx_r, xhdev)

    def arrived(line, j, p):
        for dr in range(2):
            if j == 3:
                if p == 0:
                    cz(line, dr, j, 0).wait_recv()
                    cz(line, dr, j, 1).wait_recv()
            else:
                cz(line, dr, j, p).wait_recv()

    def forward(line, j, p):
        if j > 1:
            arrived(line, j - 1, p)
        for dr in range(2):
            cz(line, dr, j, p).start()

    pltpu.make_async_copy(proj, pj.at[s], sem_proj).wait()
    cx().start()
    forward(1, 1, 0)
    forward(1, 1, 1)

    def ac(j, xo):
        return remote(a_send.at[j, xo], a_crecv.at[j, xo], ac_s.at[j, xo], ac_r.at[j, xo], sib)

    def ax(j):
        return remote(a_own.at[j, 1 - x, pl.ds(0, ROWS_A)], a_xrecv.at[j], ax_s.at[j], ax_r.at[j], xdev)

    def a_half(dr):
        return remote(
            a_own.at[0, x, pl.ds(HALF_A * dr, HALF_A)], ya_half.at[dr], ay_s.at[0, dr], ay_r.at[0, dr], ydev(1 + 2 * dr)
        )

    def a_full(dr):
        return remote(
            a_own.at[1 + dr, x, pl.ds(0, ROWS_A)], ya_full.at[dr], ay_s.at[1, dr], ay_r.at[1, dr], ydev(1 + 2 * dr)
        )

    def b_half(dr, xo):
        return remote(
            a_own.at[0, xo, pl.ds(ROWS_A + HALF_B * dr, HALF_B)], yb_half.at[dr, xo], by_s.at[0, dr, xo], by_r.at[0, dr, xo],
            ydev(1 + 2 * dr),
        )

    def b_full(dr, xo):
        return remote(
            a_own.at[1 + dr, xo, pl.ds(ROWS_A, 2 * HALF_B)], yb_full.at[dr, xo], by_s.at[1, dr, xo], by_r.at[1, dr, xo],
            ydev(1 + 2 * dr),
        )

    def bx():
        return remote(a_own.at[3, 1 - x, pl.ds(ROWS_A, 2 * HALF_B)], xb_recv, bx_s, bx_r, xdev)

    def product(j, xo, co, out):
        b = block_of(j, xo, co)
        col = pl.multiple_of(b * 512, 512)
        pltpu.make_async_copy(weight.at[:, pl.ds(col, 512)], w_v.at[b], sem_w.at[b]).wait()
        out[j, xo] = dot(attn_v[...].reshape(512, 512), w_v[b]).astype(BF16)

    def unit(u):
        return u // 2, (x + 1 + u % 2) % 2

    def multiply(u):
        j, xo = unit(u)
        product(j, xo, 1 - c, a_send)
        ac(j, xo).start()
        product(j, xo, c, a_own)

    def combine(u):
        j, xo = unit(u)
        ac(j, xo).wait_recv()
        a_own[j, xo] = (a_own[j, xo].astype(F32) + a_crecv[j, xo].astype(F32)).astype(BF16)

        @pl.when(u % 2 == 0)
        def _():
            ax(j).start()

        @pl.when(u < 2)
        def _():
            b_half(0, xo).start()
            b_half(1, xo).start()

    def send_b(dr, xo):
        rows = slice(ROWS_A + HALF_B * dr, ROWS_A + HALF_B * dr + HALF_B)
        b_half(dr, xo).wait_recv()
        a_own[1 + dr, xo, rows] = (a_own[1 + dr, xo, rows].astype(F32) + yb_half[dr, xo].astype(F32)).astype(BF16)
        b_full(dr, xo).start()

    def add_a(j):
        ax(j).wait_recv()
        a_own[j, x, 0:ROWS_A] = (a_own[j, x, 0:ROWS_A].astype(F32) + a_xrecv[j].astype(F32)).astype(BF16)

    pltpu.make_async_copy(attn, attn, sem_attn).wait()

    def teacher(u, carry):
        @pl.when(u < 8)
        def _():
            multiply(u)

        @pl.when(u >= 1)
        def _():
            combine(u - 1)

        @pl.when(u == 4)
        def _():
            forward(1, 2, 0)

        @pl.when(u == 6)
        def _():
            forward(1, 2, 1)

        @pl.when(u == 7)
        def _():
            send_b(0, 1 - x)
            send_b(1, 1 - x)

        return carry

    lax.fori_loop(0, 9, teacher, 0)

    def send_a(dr):
        rows = slice(HALF_A * dr, HALF_A * dr + HALF_A)
        add_a(1 + dr)
        a_half(dr).wait_recv()
        a_own[1 + dr, x, rows] = (a_own[1 + dr, x, rows].astype(F32) + ya_half[dr].astype(F32)).astype(BF16)
        a_full(dr).start()

    def sum_b(xo):
        b_full(0, xo).wait_recv()
        b_full(1, xo).wait_recv()
        a_own[3, xo, ROWS_A:512] = (
            a_own[3, xo, ROWS_A:512].astype(F32) + yb_full[0, xo].astype(F32) + yb_full[1, xo].astype(F32)
        ).astype(BF16)

    add_a(0)
    for dr in range(2):
        a_half(dr).start()
    for dr in range(2):
        send_b(dr, x)
    cx().wait_recv()
    forward(0, 1, 0)
    forward(0, 1, 1)
    forward(0, 2, 0)
    send_a(0)
    forward(0, 2, 1)
    send_a(1)
    sum_b(1 - x)
    bx().start()
    forward(0, 3, 0)
    forward(0, 3, 1)
    add_a(3)
    sum_b(x)
    forward(0, 4, 0)
    forward(0, 4, 1)
    forward(1, 3, 0)
    forward(1, 3, 1)
    a_full(0).wait_recv()
    a_full(1).wait_recv()
    pltpu.make_async_copy(resid, resid, sem_res).wait()

    def finish(lo, hi, total):
        hidden = total + res_v[lo // 32 : hi // 32].astype(F32).reshape(hi - lo, 512)
        hg[lo:hi] = (hidden * gain[...].astype(F32)).astype(BF16)
        sq = hidden * hidden
        sq = sq[:, 0:128] + sq[:, 128:256] + sq[:, 256:384] + sq[:, 384:512]
        pw[lo // 32 : hi // 32] = sq.reshape((hi - lo) // 32, 32, 128)

    finish(0, ROWS_A, a_own[3, x, 0:ROWS_A].astype(F32) + ya_full[0].astype(F32) + ya_full[1].astype(F32))
    bx().wait_recv()
    finish(ROWS_A, 512, a_own[3, x, ROWS_A:512].astype(F32) + xb_recv[...].astype(F32))

    def power(i):
        to = (t + i) % 16
        return remote(
            pw.at[to % 2 * 8 + to // 8 * 4 + to // 2 % 4], pw_recv.at[i], pw_s.at[i], pw_r.at[i], (s, to)
        )

    def send_power(i, carry):
        power(i).start()
        return carry

    lax.fori_loop(1, 16, send_power, 0)

    def root():
        def one(i, total):
            power(i).wait_recv()
            power(i).wait_send()
            return total + pw_recv[i]

        total = lax.fori_loop(1, 16, one, pw[c * 8 + x * 4 + y])
        mean = jnp.sum(total, axis=1, keepdims=True) * (1.0 / 8192)
        r_v[...] = jnp.broadcast_to(lax.rsqrt(mean + 1e-05), (32, 256))

    pltpu.make_async_copy(student, stu_v, sem_stu).wait()
    arrived(0, 4, 0)
    arrived(0, 4, 1)

    def block(q, m):
        line = (q + 3 + 2 * m) // 8
        off = (1 - 2 * m) * (4 - q - m + 4 * line)
        return (xh + 1 + line) % 2 * 8 + (z + off + 8) % 8

    def ds_(k, i):
        return d_s.at[k, i], d_r.at[k, i]

    def dc(k):
        return remote(t_send.at[k], t_crecv.at[k], *ds_(k, 0), sib)

    def dx(g, m):
        k = 2 * g + m
        if m == 0:
            return remote(t_own.at[k, 1 - x], xr0.at[g], *ds_(k, 1), xdev)
        return remote(t_own.at[k, 1 - x, y], xr1.at[g], *ds_(k, 1), xdev)

    def dy(g, m, o):
        k = 2 * g + m
        if m == 0:
            return remote(t_own.at[k, x, (y + o) % 4], yr0.at[g, o - 1], *ds_(k, 1 + o), ydev(o))
        return remote(t_own.at[k, :, (y + o) % 4], yr1.at[g, o - 1], *ds_(k, 1 + o), ydev(o))

    def ex(g, m):
        k = 2 * g + m
        ref = m_all.at[k, c, x] if m == 0 else m_all.at[k, c, x, y]
        return remote(ref, ref, *ds_(k, 5), xdev)

    def ey(g, m, o):
        k = 2 * g + m
        ref = m_all.at[k, c, x, y] if m == 0 else m_all.at[k, c, :, y]
        return remote(ref, ref, *ds_(k, 5 + o), ydev(o))

    def ec(k):
        return remote(m_all.at[k, c], m_all.at[k, c], *ds_(k, 9), sib)

    def fz(line, dr, j, p, k):
        cols = pl.ds(256 * p, 256)
        return remote(
            g_send.at[k, :, cols], ring.at[line, dr, j, :, cols], f_s.at[line, dr, j, p], f_r.at[line, dr, j, p],
            zdev[dr],
        )

    def fz_half(line, dr, p, k):
        rows, cols = pl.ds(128 * dr, 128), pl.ds(256 * p, 256)
        return remote(
            g_send.at[k, rows, cols], ring.at[line, dr, 0, rows, cols], f_s.at[line, dr, 0, p],
            f_r.at[line, dr, 0, p], zdev[dr],
        )

    def fx(p):
        cols = pl.ds(256 * p, 256)
        return remote(g_send.at[8, :, cols], rx.at[:, cols], fx_s.at[p], fx_r.at[p], xhdev)

    def core_rows(co):
        return pl.ds(pl.multiple_of(co * 256, 256), 256)

    def stage0(g, m):
        k = 2 * g + m
        b = block(g, m)
        t_send[k] = dot(hg[core_rows(1 - c)], pj[b]).astype(BF16).reshape(2, 4, 32, 256)
        dc(k).start()
        t_own[k] = dot(hg[core_rows(c)], pj[b]).astype(BF16).reshape(2, 4, 32, 256)

    def stage1(g, m):
        k = 2 * g + m
        dc(k).wait_recv()
        t_own[k] = (t_own[k].astype(F32) + t_crecv[k].astype(F32)).astype(BF16)
        if m == 0:
            dx(g, m).start()
        else:
            for o in (2, 1, 3):
                dy(g, m, o).start()

    def stage2(g, m):
        k = 2 * g + m
        dc(k).wait_send()
        if m == 0:
            dx(g, m).wait_recv()
            t_own[k, x] = (t_own[k, x].astype(F32) + xr0[g].astype(F32)).astype(BF16)
            for o in (2, 1, 3):
                dy(g, m, o).start()
        else:
            total = t_own[k, :, y].astype(F32)
            for o in (1, 2, 3):
                dy(g, m, o).wait_recv()
                total = total + yr1[g, o - 1].astype(F32)
            t_own[k, :, y] = total.astype(BF16)
            dx(g, m).start()

    def stage3(g, m):
        k = 2 * g + m
        if m == 0:
            total = t_own[k, x, y].astype(F32)
            for o in (1, 2, 3):
                dy(g, m, o).wait_recv()
                total = total + yr0[g, o - 1].astype(F32)
        else:
            dx(g, m).wait_recv()
            total = t_own[k, x, y].astype(F32) + xr1[g].astype(F32)
        cols = pl.ds(pl.multiple_of(block(g, m) * 256, 256), 256)
        mismatch = total * r_v[...] - stu_v[:, cols].astype(F32)
        mis_v[:, cols] = mismatch
        m_all[k, c, x, y] = (mismatch * r_v[...]).astype(BF16)
        if m == 0:
            for o in (2, 1, 3):
                ey(g, m, o).start()
        else:
            ex(g, m).start()
        dx(g, m).wait_send()
        for o in (1, 2, 3):
            dy(g, m, o).wait_send()

    def stage4(g, m):
        if m == 0:
            for o in (1, 2, 3):
                ey(g, m, o).wait_recv()
            ex(g, m).start()
        else:
            ex(g, m).wait_recv()
            for o in (2, 1, 3):
                ey(g, m, o).start()

    def stage5(g, m):
        if m == 0:
            ex(g, m).wait_recv()
        else:
            for o in (1, 2, 3):
                ey(g, m, o).wait_recv()
        ec(2 * g + m).start()
        ex(g, m).wait_send()
        for o in (1, 2, 3):
            ey(g, m, o).wait_send()

    def put_grad(p):
        cols = pl.ds(256 * p, 256)
        return pltpu.make_async_copy(grad_v.at[:, cols], grad_out.at[:, cols], sem_grad.at[p])

    def put_mis():
        return pltpu.make_async_copy(mis_v, mis_out, sem_mis)

    def stage6(q, m):
        k = 2 * q + m
        ec(k).wait_recv()
        g_acc[m] = dot(m_all[k].reshape(512, 256), hg[...], ((0,), (0,)))
        ec(k).wait_send()
        reduce(q, m, 0)

    def stage7(q, m):
        reduce(q, m, 1)

    def reduce(q, m, p):
        k = 2 * q + m
        cols = slice(256 * p, 256 * p + 256)
        part = g_acc[m, :, cols]

        @pl.when(q == 3 * m)
        def _():
            g_send[k, :, cols] = part.astype(BF16)
            fz_half(m, 0, p, k).start()
            fz_half(m, 1, p, k).start()

        @pl.when(q == 4 + 3 * m)
        def _():
            for dr in range(2):
                fz(m, dr, 3, p, k).wait_recv()
            total = part + ring[m, 0, 3, :, cols].astype(F32) + ring[m, 1, 3, :, cols].astype(F32)
            if m == 0:
                g_send[k, :, cols] = total.astype(BF16)
                fx(p).start()
            else:
                fx(p).wait_recv()
                grad_v[:, cols] = (total + rx[:, cols].astype(F32)) * (1.0 / math.sqrt(8192))
                put_grad(p).start()

        @pl.when((q != 3 * m) & (q != 4 + 3 * m))
        def _():
            line = (q + 3 + 2 * m) // 8
            j = q + m - 1 - 4 * line

            @pl.when(j == 0)
            def _():
                fz_half(line, m, p, k).wait_recv()

            @pl.when(j > 0)
            def _():
                fz(line, m, j, p, k).wait_recv()

            g_send[k, :, cols] = (part + ring[line, m, j, :, cols].astype(F32)).astype(BF16)
            fz(line, m, j + 1, p, k).start()

    stages = (stage0, stage1, stage2, stage3, stage4, stage5, stage6, stage7)

    def student_steps(h, carry):
        for par in range(2):
            for n in reversed(range(len(stages))):
                m = (par - STEPS[n]) % 2
                q = h + (par - STEPS[n] - m) // 2
                pl.when((q >= 0) & (q < BLOCKS))(lambda: stages[n](q, m))

            if par == 0:

                @pl.when(h == 2)
                def _():
                    root()
                    forward(1, 4, 0)
                    forward(1, 4, 1)

                @pl.when(h == 3)
                def _():
                    arrived(1, 4, 0)
                    arrived(1, 4, 1)

                @pl.when(h == 11)
                def _():
                    put_mis().start()

        return carry

    lax.fori_loop(0, BLOCKS + (STEPS[-1] + 1) // 2, student_steps, 0)

    cx().wait_send()
    for line in range(2):
        for dr in range(2):
            for j in range(1, 5):
                cz(line, dr, j, 0).wait_send()
                cz(line, dr, j, 1).wait_send()
            for p in range(2):
                fz_half(line, dr, p, 0).wait_send()
                for j in range(1, 4):
                    fz(line, dr, j, p, 0).wait_send()
    for j in range(4):
        for xo in range(2):
            ac(j, xo).wait_send()
        ax(j).wait_send()
    for dr in range(2):
        a_half(dr).wait_send()
        a_full(dr).wait_send()
        for xo in range(2):
            b_half(dr, xo).wait_send()
            b_full(dr, xo).wait_send()
    bx().wait_send()
    fx(0).wait_send()
    fx(1).wait_send()
    put_mis().wait()
    put_grad(0).wait()
    put_grad(1).wait()


def shards(attn_heads, out_weight, residual, norm_gain, proj, student_hidden):
    hbm = pl.BlockSpec(memory_space=pl.ANY)
    vmem = pl.BlockSpec(memory_space=pltpu.VMEM)
    buf = lambda *shape: pltpu.VMEM(shape, BF16)
    dma = lambda *shape: pltpu.SemaphoreType.DMA(shape)
    return pl.pallas_call(
        kernel,
        name="distill",
        out_shape=(
            jax.ShapeDtypeStruct((32, 4096), F32),
            jax.ShapeDtypeStruct((256, 512), F32),
        ),
        in_specs=[hbm, hbm, hbm, vmem, hbm, hbm],
        out_specs=(hbm, hbm),
        scratch_shapes=[
            buf(16, 32, 512), buf(16, 32, 512), buf(16, 512, 512), buf(32, 4096),
            buf(4, 2, 512, 512), buf(4, 2, 512, 512), buf(4, 2, 512, 512), buf(4, ROWS_A, 512),
            buf(2, HALF_A, 512), buf(2, ROWS_A, 512), buf(2, 2, HALF_B, 512), buf(2, 2, 2 * HALF_B, 512),
            buf(2 * HALF_B, 512),
            buf(512, 512), pltpu.VMEM((16, 32, 128), F32), pltpu.VMEM((16, 32, 128), F32),
            pltpu.VMEM((32, 256), F32),
            buf(16, 512, 256),
            buf(16, 2, 4, 32, 256), buf(16, 2, 4, 32, 256), buf(16, 2, 4, 32, 256),
            buf(8, 4, 32, 256), buf(8, 3, 32, 256), buf(8, 3, 2, 32, 256), buf(8, 32, 256),
            buf(16, 2, 2, 4, 32, 256),
            pltpu.VMEM((2, 256, 512), F32), buf(16, 256, 512), buf(2, 2, 4, 256, 512), buf(256, 512),
            pltpu.VMEM((32, 4096), F32), pltpu.VMEM((256, 512), F32),
            dma(), dma(), dma(), dma(16), dma(), dma(), dma(2),
            dma(4, 2), dma(4, 2), dma(4), dma(4), dma(2, 2), dma(2, 2), dma(2, 2, 2), dma(2, 2, 2), dma(), dma(),
            dma(16), dma(16), dma(), dma(), dma(2, 2, 4, 2), dma(2, 2, 4, 2),
            dma(16, 10), dma(16, 10), dma(2, 2, 4, 2), dma(2, 2, 4, 2), dma(2), dma(2),
        ],
        compiler_params=pltpu.CompilerParams(
            collective_id=0, has_side_effects=True, vmem_limit_bytes=62 * 2**20
        ),
    )(attn_heads, out_weight, residual, norm_gain.reshape(1, 512), proj, student_hidden)


def solution(mesh):
    return jax.shard_map(
        shards,
        mesh=mesh,
        in_specs=(
            P("seq", "tensor"),
            P("tensor", None),
            P("seq", "tensor"),
            P("tensor"),
            P("tensor", "seq"),
            P(("seq", "tensor"), None),
        ),
        out_specs=(P(("seq", "tensor"), None), P("seq", "tensor")),
        check_vma=False,
    )
```

time: 130 us -> 125 us (0.962)
  Pallas kernels: 124 us -> 118 us
    pallas_call x1, Pallas kernels: 124 us -> 118 us  [shards(): pl.pallas_call(kernel, name='distill', out_shape=(jax.ShapeDtypeStruct((3...]
where the time goes in v2:
time: 125 us; the launch traced here: 124 us
  Pallas kernels  118 us (94%)
  local copies, waits for them, and re-layouts  5 us (4%)
    pallas_call x1, Pallas kernels, shards(): pl.pallas_call(kernel, name='distill', out_shape=(jax.ShapeDtypeStruct((3...  118 us
    unnamed x2, local copies, waits for them, and re-layouts  3.74 us

profile of v2, /device:TPU:8, one launch (start us, length us, event | category | flops | bytes accessed | tf_op | source)
XLA Modules:
  0.0 123.6 jit_solution(12386353236336642600)
XLA Ops:
  0.6 1.3 %reshape.7.gain = bf16[1,512]{1,0:T(2,128)(2,1)} reshape(bf16[512]{0:T(512)(128)(2,1)} %param.9) | data formatting | bytes 2048 | tf_op jit(solution)/shard_map/reshape | solution.py:596
  1.9 118.0 %distill.1 = (f32[32,4096]{1,0:T(8,128)}, f32[256,512]{1,0:T(8,128)}) custom-call(bf16[512,512]{1,0:T(8,128)(2,1)} %attn.1, bf16[512,8192]{1,0:T(8,128)(2,1)} %weight.1, bf16[512,512]{1,0:T(8,128)(2,1)} %resid.1, bf16[1,512]{1,0:T(2,128)(2,1)} %reshape.7.gain, bf16[512,256]{1,0:T(8,128)(2,1)} %proj.1, bf16[32,4096]{1,0:T(8,128)(2,1)} %student.1), custom_call_target="tpu_custom_call" | custom-call | tf_op jit(solution)/shard_map/distill/pallas_call | solution.py:566
  119.9 1.9 %copy.10 = f32[32,4096]{1,0:T(8,128)} copy(f32[32,4096]{1,0:T(8,128)} %get-tuple-element.4) | data formatting | bytes 1048576
  121.8 1.9 %copy.11 = f32[256,512]{1,0:T(8,128)} copy(f32[256,512]{1,0:T(8,128)} %get-tuple-element.5) | data formatting | bytes 1048576

commit v3 on v2

--- a/solution.py
+++ b/solution.py
@@ -65,6 +65,9 @@
     for dev in (xhdev,) + zdev:
         pl.semaphore_signal(barrier, inc=1, device_id=dev, device_id_type=MESH)
 
+    def whole(ref, ss, rs):
+        return remote(ref, ref, ss, rs, sib)
+
     def tokens(i):
         return (i % 8) // 4 * 8 + (i % 4) * 2 + i // 8
 
@@ -80,19 +83,15 @@
         dy = 2 - j + (j // 2) * (3 - 2 * (j % 2))
         return xo * 8 + (y + dy) % 4 * 2 + co
 
-    def load_w(j):
-        def one(i, carry):
-            b = block_of(j, (x + 1 + i % 2) % 2, (c + 1 + i // 2) % 2)
-            col = pl.multiple_of(b * 512, 512)
-            pltpu.make_async_copy(weight.at[:, pl.ds(col, 512)], w_v.at[b], sem_w.at[b]).start()
-            return carry
-
-        lax.fori_loop(0, 4, one, 0)
+    def load_w(u):
+        b = block_of(u // 2, (x + 1 + u % 2) % 2, 0) // 2
+        col = pl.multiple_of(b * 1024, 1024)
+        return pltpu.make_async_copy(weight.at[:, pl.ds(col, 1024)], w_v.at[u], sem_w.at[u])
 
     pltpu.make_async_copy(proj, pj.at[s], sem_proj).start()
     load_rows(attn, attn_v, sem_attn)
-    for j in range(4):
-        load_w(j)
+    for u in range(8):
+        load_w(u).start()
     load_rows(resid, res_v, sem_res)
     pltpu.make_async_copy(student, stu_v, sem_stu).start()
 
@@ -109,7 +108,7 @@
             ref = pj.at[b, pl.ds(256 * dr + 128 * p, 128)]
         else:
             ref = pj.at[b, pl.ds(256 * p, 256)]
-        return remote(ref, ref, cz_s.at[line, dr, j - 1, p], cz_r.at[line, dr, j - 1, p], zdev[dr])
+        return remote(ref, ref, cz_s, cz_r.at[line, dr, j - 1, p], zdev[dr])
 
     def cx():
         return remote(pj.at[s], pj.at[s], cx_s, cx_r, xhdev)
@@ -135,50 +134,50 @@
     forward(1, 1, 1)
 
     def ac(j, xo):
-        return remote(a_send.at[j, xo], a_crecv.at[j, xo], ac_s.at[j, xo], ac_r.at[j, xo], sib)
+        return remote(a_send.at[j, xo], a_crecv.at[j, xo], ac_s, ac_r.at[j, xo], sib)
 
     def ax(j):
-        return remote(a_own.at[j, 1 - x, pl.ds(0, ROWS_A)], a_xrecv.at[j], ax_s.at[j], ax_r.at[j], xdev)
+        return remote(a_own.at[j, 1 - x, pl.ds(0, ROWS_A)], a_xrecv.at[j], ax_s, ax_r.at[j], xdev)
 
     def a_half(dr):
         return remote(
-            a_own.at[0, x, pl.ds(HALF_A * dr, HALF_A)], ya_half.at[dr], ay_s.at[0, dr], ay_r.at[0, dr], ydev(1 + 2 * dr)
+            a_own.at[0, x, pl.ds(HALF_A * dr, HALF_A)], ya_half.at[dr], ay_s.at[0], ay_r.at[0, dr], ydev(1 + 2 * dr)
         )
 
     def a_full(dr):
         return remote(
-            a_own.at[1 + dr, x, pl.ds(0, ROWS_A)], ya_full.at[dr], ay_s.at[1, dr], ay_r.at[1, dr], ydev(1 + 2 * dr)
+            a_own.at[1 + dr, x, pl.ds(0, ROWS_A)], ya_full.at[dr], ay_s.at[1], ay_r.at[1, dr], ydev(1 + 2 * dr)
         )
 
     def b_half(dr, xo):
         return remote(
-            a_own.at[0, xo, pl.ds(ROWS_A + HALF_B * dr, HALF_B)], yb_half.at[dr, xo], by_s.at[0, dr, xo], by_r.at[0, dr, xo],
+            a_own.at[0, xo, pl.ds(ROWS_A + HALF_B * dr, HALF_B)], yb_half.at[dr, xo], by_s.at[0], by_r.at[0, dr, xo],
             ydev(1 + 2 * dr),
         )
 
     def b_full(dr, xo):
         return remote(
-            a_own.at[1 + dr, xo, pl.ds(ROWS_A, 2 * HALF_B)], yb_full.at[dr, xo], by_s.at[1, dr, xo], by_r.at[1, dr, xo],
+            a_own.at[1 + dr, xo, pl.ds(ROWS_A, 2 * HALF_B)], yb_full.at[dr, xo], by_s.at[1], by_r.at[1, dr, xo],
             ydev(1 + 2 * dr),
         )
 
     def bx():
         return remote(a_own.at[3, 1 - x, pl.ds(ROWS_A, 2 * HALF_B)], xb_recv, bx_s, bx_r, xdev)
 
-    def product(j, xo, co, out):
-        b = block_of(j, xo, co)
-        col = pl.multiple_of(b * 512, 512)
-        pltpu.make_async_copy(weight.at[:, pl.ds(col, 512)], w_v.at[b], sem_w.at[b]).wait()
-        out[j, xo] = dot(attn_v[...].reshape(512, 512), w_v[b]).astype(BF16)
+    def product(u, co, out):
+        j, xo = unit(u)
+        cols = pl.ds(pl.multiple_of(co * 512, 512), 512)
+        out[j, xo] = dot(attn_v[...].reshape(512, 512), w_v[u, :, cols]).astype(BF16)
 
     def unit(u):
         return u // 2, (x + 1 + u % 2) % 2
 
     def multiply(u):
         j, xo = unit(u)
-        product(j, xo, 1 - c, a_send)
+        load_w(u).wait()
+        product(u, 1 - c, a_send)
         ac(j, xo).start()
-        product(j, xo, c, a_own)
+        product(u, c, a_own)
 
     def combine(u):
         j, xo = unit(u)
@@ -215,18 +214,17 @@
         def _():
             combine(u - 1)
 
-        @pl.when(u == 4)
+        @pl.when(u == 6)
         def _():
             forward(1, 2, 0)
-
-        @pl.when(u == 6)
-        def _():
-            forward(1, 2, 1)
 
         @pl.when(u == 7)
         def _():
             send_b(0, 1 - x)
             send_b(1, 1 - x)
+            cx().wait_recv()
+            forward(0, 1, 0)
+            forward(0, 1, 1)
 
         return carry
 
@@ -251,30 +249,27 @@
         a_half(dr).start()
     for dr in range(2):
         send_b(dr, x)
-    cx().wait_recv()
-    forward(0, 1, 0)
-    forward(0, 1, 1)
     forward(0, 2, 0)
-    send_a(0)
     forward(0, 2, 1)
-    send_a(1)
     sum_b(1 - x)
     bx().start()
     forward(0, 3, 0)
+    send_a(0)
+    send_a(1)
     forward(0, 3, 1)
     add_a(3)
-    sum_b(x)
     forward(0, 4, 0)
     forward(0, 4, 1)
+    forward(1, 2, 1)
     forward(1, 3, 0)
-    forward(1, 3, 1)
+    sum_b(x)
     a_full(0).wait_recv()
     a_full(1).wait_recv()
     pltpu.make_async_copy(resid, resid, sem_res).wait()
 
     def finish(lo, hi, total):
         hidden = total + res_v[lo // 32 : hi // 32].astype(F32).reshape(hi - lo, 512)
-        hg[lo:hi] = (hidden * gain[...].astype(F32)).astype(BF16)
+        hg[lo:hi] = (hidden * gain[...].astype(F32).reshape(1, 512)).astype(BF16)
         sq = hidden * hidden
         sq = sq[:, 0:128] + sq[:, 128:256] + sq[:, 256:384] + sq[:, 384:512]
         pw[lo // 32 : hi // 32] = sq.reshape((hi - lo) // 32, 32, 128)
@@ -286,7 +281,7 @@
     def power(i):
         to = (t + i) % 16
         return remote(
-            pw.at[to % 2 * 8 + to // 8 * 4 + to // 2 % 4], pw_recv.at[i], pw_s.at[i], pw_r.at[i], (s, to)
+            pw.at[to % 2 * 8 + to // 8 * 4 + to // 2 % 4], pw_recv.at[i], pw_s, pw_r, (s, to)
         )
 
     def send_power(i, carry):
@@ -296,9 +291,9 @@
     lax.fori_loop(1, 16, send_power, 0)
 
     def root():
+        whole(pw_recv.at[pl.ds(1, 15)], pw_s, pw_r).wait_recv()
+
         def one(i, total):
-            power(i).wait_recv()
-            power(i).wait_send()
             return total + pw_recv[i]
 
         total = lax.fori_loop(1, 16, one, pw[c * 8 + x * 4 + y])
@@ -315,7 +310,7 @@
         return (xh + 1 + line) % 2 * 8 + (z + off + 8) % 8
 
     def ds_(k, i):
-        return d_s.at[k, i], d_r.at[k, i]
+        return d_s.at[k % 2, i], d_r.at[k % 8, i]
 
     def dc(k):
         return remote(t_send.at[k], t_crecv.at[k], *ds_(k, 0), sib)
@@ -329,39 +324,42 @@
     def dy(g, m, o):
         k = 2 * g + m
         if m == 0:
-            return remote(t_own.at[k, x, (y + o) % 4], yr0.at[g, o - 1], *ds_(k, 1 + o), ydev(o))
-        return remote(t_own.at[k, :, (y + o) % 4], yr1.at[g, o - 1], *ds_(k, 1 + o), ydev(o))
+            return remote(t_own.at[k, x, (y + o) % 4], yr0.at[g, o - 1], *ds_(k, 2), ydev(o))
+        return remote(t_own.at[k, :, (y + o) % 4], yr1.at[g, o - 1], *ds_(k, 2), ydev(o))
 
     def ex(g, m):
         k = 2 * g + m
         ref = m_all.at[k, c, x] if m == 0 else m_all.at[k, c, x, y]
-        return remote(ref, ref, *ds_(k, 5), xdev)
+        return remote(ref, ref, *ds_(k, 3), xdev)
 
     def ey(g, m, o):
         k = 2 * g + m
         ref = m_all.at[k, c, x, y] if m == 0 else m_all.at[k, c, :, y]
-        return remote(ref, ref, *ds_(k, 5 + o), ydev(o))
+        return remote(ref, ref, *ds_(k, 4), ydev(o))
+
+    def y_arrived(g, m, i):
+        whole(yr0.at[g] if m == 0 else yr1.at[g], *ds_(2 * g + m, i)).wait_recv()
 
     def ec(k):
-        return remote(m_all.at[k, c], m_all.at[k, c], *ds_(k, 9), sib)
+        return remote(m_all.at[k, c], m_all.at[k, c], *ds_(k, 5), sib)
 
     def fz(line, dr, j, p, k):
         cols = pl.ds(256 * p, 256)
         return remote(
-            g_send.at[k, :, cols], ring.at[line, dr, j, :, cols], f_s.at[line, dr, j, p], f_r.at[line, dr, j, p],
+            g_send.at[k, :, cols], ring.at[line, dr, j, :, cols], f_s, f_r.at[line, dr, j, p],
             zdev[dr],
         )
 
     def fz_half(line, dr, p, k):
         rows, cols = pl.ds(128 * dr, 128), pl.ds(256 * p, 256)
         return remote(
-            g_send.at[k, rows, cols], ring.at[line, dr, 0, rows, cols], f_s.at[line, dr, 0, p],
+            g_send.at[k, rows, cols], ring.at[line, dr, 0, rows, cols], f_s,
             f_r.at[line, dr, 0, p], zdev[dr],
         )
 
     def fx(p):
         cols = pl.ds(256 * p, 256)
-        return remote(g_send.at[8, :, cols], rx.at[:, cols], fx_s.at[p], fx_r.at[p], xhdev)
+        return remote(g_send.at[8, :, cols], rx.at[:, cols], fx_s, fx_r.at[p], xhdev)
 
     def core_rows(co):
         return pl.ds(pl.multiple_of(co * 256, 256), 256)
@@ -385,7 +383,6 @@
 
     def stage2(g, m):
         k = 2 * g + m
-        dc(k).wait_send()
         if m == 0:
             dx(g, m).wait_recv()
             t_own[k, x] = (t_own[k, x].astype(F32) + xr0[g].astype(F32)).astype(BF16)
@@ -393,9 +390,9 @@
                 dy(g, m, o).start()
         else:
             total = t_own[k, :, y].astype(F32)
-            for o in (1, 2, 3):
-                dy(g, m, o).wait_recv()
-                total = total + yr1[g, o - 1].astype(F32)
+            y_arrived(g, m, 2)
+            for o in range(3):
+                total = total + yr1[g, o].astype(F32)
             t_own[k, :, y] = total.astype(BF16)
             dx(g, m).start()
 
@@ -403,9 +400,9 @@
         k = 2 * g + m
         if m == 0:
             total = t_own[k, x, y].astype(F32)
-            for o in (1, 2, 3):
-                dy(g, m, o).wait_recv()
-                total = total + yr0[g, o - 1].astype(F32)
+            y_arrived(g, m, 2)
+            for o in range(3):
+                total = total + yr0[g, o].astype(F32)
         else:
             dx(g, m).wait_recv()
             total = t_own[k, x, y].astype(F32) + xr1[g].astype(F32)
@@ -418,14 +415,10 @@
                 ey(g, m, o).start()
         else:
             ex(g, m).start()
-        dx(g, m).wait_send()
-        for o in (1, 2, 3):
-            dy(g, m, o).wait_send()
 
     def stage4(g, m):
         if m == 0:
-            for o in (1, 2, 3):
-                ey(g, m, o).wait_recv()
+            y_arrived(g, m, 4)
             ex(g, m).start()
         else:
             ex(g, m).wait_recv()
@@ -436,12 +429,8 @@
         if m == 0:
             ex(g, m).wait_recv()
         else:
-            for o in (1, 2, 3):
-                ey(g, m, o).wait_recv()
+            y_arrived(g, m, 4)
         ec(2 * g + m).start()
-        ex(g, m).wait_send()
-        for o in (1, 2, 3):
-            ey(g, m, o).wait_send()
 
     def put_grad(p):
         cols = pl.ds(256 * p, 256)
@@ -454,7 +443,6 @@
         k = 2 * q + m
         ec(k).wait_recv()
         g_acc[m] = dot(m_all[k].reshape(512, 256), hg[...], ((0,), (0,)))
-        ec(k).wait_send()
         reduce(q, m, 0)
 
     def stage7(q, m):
@@ -511,6 +499,10 @@
 
             if par == 0:
 
+                @pl.when(h == 0)
+                def _():
+                    forward(1, 3, 1)
+
                 @pl.when(h == 2)
                 def _():
                     root()
@@ -530,29 +522,16 @@
 
     lax.fori_loop(0, BLOCKS + (STEPS[-1] + 1) // 2, student_steps, 0)
 
-    cx().wait_send()
-    for line in range(2):
-        for dr in range(2):
-            for j in range(1, 5):
-                cz(line, dr, j, 0).wait_send()
-                cz(line, dr, j, 1).wait_send()
-            for p in range(2):
-                fz_half(line, dr, p, 0).wait_send()
-                for j in range(1, 4):
-                    fz(line, dr, j, p, 0).wait_send()
-    for j in range(4):
-        for xo in range(2):
-            ac(j, xo).wait_send()
-        ax(j).wait_send()
-    for dr in range(2):
-        a_half(dr).wait_send()
-        a_full(dr).wait_send()
-        for xo in range(2):
-            b_half(dr, xo).wait_send()
-            b_full(dr, xo).wait_send()
-    bx().wait_send()
-    fx(0).wait_send()
-    fx(1).wait_send()
+    for ref, sem in (
+        (pj.at[s], cx_s), (pj.at[pl.ds(0, 14)], cz_s), (a_send, ac_s), (a_xrecv, ax_s), (ya_half, ay_s.at[0]),
+        (ya_full, ay_s.at[1]), (yb_half, by_s.at[0]), (yb_full, by_s.at[1]), (xb_recv, bx_s),
+        (pw_recv.at[pl.ds(1, 15)], pw_s), (g_send.at[pl.ds(0, 14)], f_s), (rx, fx_s),
+        (t_send.at[pl.ds(0, 8)], d_s.at[0, 0]), (t_send.at[pl.ds(0, 8)], d_s.at[1, 0]),
+        (xr0, d_s.at[0, 1]), (xr1, d_s.at[1, 1]), (yr0, d_s.at[0, 2]), (yr1, d_s.at[1, 2]),
+        (xr0, d_s.at[0, 3]), (xr1, d_s.at[1, 3]), (yr0, d_s.at[0, 4]), (yr1, d_s.at[1, 4]),
+        (t_send.at[pl.ds(0, 8)], d_s.at[0, 5]), (t_send.at[pl.ds(0, 8)], d_s.at[1, 5]),
+    ):
+        whole(ref, sem, pw_r).wait_send()
     put_mis().wait()
     put_grad(0).wait()
     put_grad(1).wait()
@@ -573,7 +552,7 @@
         in_specs=[hbm, hbm, hbm, vmem, hbm, hbm],
         out_specs=(hbm, hbm),
         scratch_shapes=[
-            buf(16, 32, 512), buf(16, 32, 512), buf(16, 512, 512), buf(32, 4096),
+            buf(16, 32, 512), buf(16, 32, 512), buf(8, 512, 1024), buf(32, 4096),
             buf(4, 2, 512, 512), buf(4, 2, 512, 512), buf(4, 2, 512, 512), buf(4, ROWS_A, 512),
             buf(2, HALF_A, 512), buf(2, ROWS_A, 512), buf(2, 2, HALF_B, 512), buf(2, 2, 2 * HALF_B, 512),
             buf(2 * HALF_B, 512),
@@ -585,15 +564,15 @@
             buf(16, 2, 2, 4, 32, 256),
             pltpu.VMEM((2, 256, 512), F32), buf(16, 256, 512), buf(2, 2, 4, 256, 512), buf(256, 512),
             pltpu.VMEM((32, 4096), F32), pltpu.VMEM((256, 512), F32),
-            dma(), dma(), dma(), dma(16), dma(), dma(), dma(2),
-            dma(4, 2), dma(4, 2), dma(4), dma(4), dma(2, 2), dma(2, 2), dma(2, 2, 2), dma(2, 2, 2), dma(), dma(),
-            dma(16), dma(16), dma(), dma(), dma(2, 2, 4, 2), dma(2, 2, 4, 2),
-            dma(16, 10), dma(16, 10), dma(2, 2, 4, 2), dma(2, 2, 4, 2), dma(2), dma(2),
+            dma(), dma(), dma(), dma(8), dma(), dma(), dma(2),
+            dma(), dma(4, 2), dma(), dma(4), dma(2), dma(2, 2), dma(2), dma(2, 2, 2), dma(), dma(),
+            dma(), dma(), dma(), dma(), dma(), dma(2, 2, 4, 2),
+            dma(2, 6), dma(8, 6), dma(), dma(2, 2, 4, 2), dma(), dma(2),
         ],
         compiler_params=pltpu.CompilerParams(
             collective_id=0, has_side_effects=True, vmem_limit_bytes=62 * 2**20
         ),
-    )(attn_heads, out_weight, residual, norm_gain.reshape(1, 512), proj, student_hidden)
+    )(attn_heads, out_weight, residual, norm_gain, proj, student_hidden)
 
 
 def solution(mesh):

time: 125 us -> 119 us (0.952)
  Pallas kernels: 118 us -> 114 us
  local copies, waits for them, and re-layouts: 5 us -> 3.74 us
    pallas_call x1, Pallas kernels: 118 us -> 114 us  [shards(): pl.pallas_call(kernel, name='distill', out_shape=(jax.ShapeDtypeStruct((3...]
    reshape x1 -> x0, local copies, waits for them, and re-layouts: 1.26 us -> none  [shards(): norm_gain.reshape(1, 512)]
where the time goes in v3:
time: 119 us; the launch traced here: 118 us
  Pallas kernels  114 us (96%)
  local copies, waits for them, and re-layouts  3.74 us (3%)
    pallas_call x1, Pallas kernels, shards(): pl.pallas_call(kernel, name='distill', out_shape=(jax.ShapeDtypeStruct((3...  114 us
    unnamed x2, local copies, waits for them, and re-layouts  3.74 us

profile of v3, /device:TPU:8, one launch (start us, length us, event | category | flops | bytes accessed | tf_op | source)
XLA Modules:
  0.0 118.1 jit_solution(10666771462123840715)
XLA Ops:
  0.6 113.7 %distill.1 = (f32[32,4096]{1,0:T(8,128)}, f32[256,512]{1,0:T(8,128)}) custom-call(bf16[512,512]{1,0:T(8,128)(2,1)} %attn.1, bf16[512,8192]{1,0:T(8,128)(2,1)} %weight.1, bf16[512,512]{1,0:T(8,128)(2,1)} %resid.1, bf16[512]{0:T(512)(128)(2,1)} %gain.1, bf16[512,256]{1,0:T(8,128)(2,1)} %proj.1, bf16[32,4096]{1,0:T(8,128)(2,1)} %student.1), custom_call_target="tpu_custom_call" | custom-call | tf_op jit(solution)/shard_map/distill/pallas_call | solution.py:545
  114.3 1.9 %copy.10 = f32[32,4096]{1,0:T(8,128)} copy(f32[32,4096]{1,0:T(8,128)} %get-tuple-element.4) | data formatting | bytes 1048576
  116.2 1.9 %copy.11 = f32[256,512]{1,0:T(8,128)} copy(f32[256,512]{1,0:T(8,128)} %get-tuple-element.5) | data formatting | bytes 1048576

commit v4 on v3

--- a/solution.py
+++ b/solution.py
@@ -28,8 +28,8 @@
     hg, pw, pw_recv, r_v,
     pj,
     t_send, t_own, t_crecv, xr0, yr0, yr1, xr1, m_all,
-    g_acc, g_send, ring, rx, mis_v, grad_v,
-    sem_attn, sem_res, sem_stu, sem_w, sem_proj, sem_mis, sem_grad,
+    g_acc, g_send, ring, rx,
+    sem_attn, sem_res, sem_stu, sem_w, sem_proj,
     ac_s, ac_r, ax_s, ax_r, ay_s, ay_r, by_s, by_r, bx_s, bx_r,
     pw_s, pw_r, cx_s, cx_r, cz_s, cz_r,
     d_s, d_r, f_s, f_r, fx_s, fx_r,
@@ -408,7 +408,7 @@
             total = t_own[k, x, y].astype(F32) + xr1[g].astype(F32)
         cols = pl.ds(pl.multiple_of(block(g, m) * 256, 256), 256)
         mismatch = total * r_v[...] - stu_v[:, cols].astype(F32)
-        mis_v[:, cols] = mismatch
+        mis_out[:, cols] = mismatch
         m_all[k, c, x, y] = (mismatch * r_v[...]).astype(BF16)
         if m == 0:
             for o in (2, 1, 3):
@@ -431,13 +431,6 @@
         else:
             y_arrived(g, m, 4)
         ec(2 * g + m).start()
-
-    def put_grad(p):
-        cols = pl.ds(256 * p, 256)
-        return pltpu.make_async_copy(grad_v.at[:, cols], grad_out.at[:, cols], sem_grad.at[p])
-
-    def put_mis():
-        return pltpu.make_async_copy(mis_v, mis_out, sem_mis)
 
     def stage6(q, m):
         k = 2 * q + m
@@ -469,8 +462,7 @@
                 fx(p).start()
             else:
                 fx(p).wait_recv()
-                grad_v[:, cols] = (total + rx[:, cols].astype(F32)) * (1.0 / math.sqrt(8192))
-                put_grad(p).start()
+                grad_out[:, cols] = (total + rx[:, cols].astype(F32)) * (1.0 / math.sqrt(8192))
 
         @pl.when((q != 3 * m) & (q != 4 + 3 * m))
         def _():
@@ -513,10 +505,6 @@
                 def _():
                     arrived(1, 4, 0)
                     arrived(1, 4, 1)
-
-                @pl.when(h == 11)
-                def _():
-                    put_mis().start()
 
         return carry
 
@@ -532,9 +520,6 @@
         (t_send.at[pl.ds(0, 8)], d_s.at[0, 5]), (t_send.at[pl.ds(0, 8)], d_s.at[1, 5]),
     ):
         whole(ref, sem, pw_r).wait_send()
-    put_mis().wait()
-    put_grad(0).wait()
-    put_grad(1).wait()
 
 
 def shards(attn_heads, out_weight, residual, norm_gain, proj, student_hidden):
@@ -546,11 +531,11 @@
         kernel,
         name="distill",
         out_shape=(
-            jax.ShapeDtypeStruct((32, 4096), F32),
-            jax.ShapeDtypeStruct((256, 512), F32),
+            pltpu.VMEM((32, 4096), F32),
+            pltpu.VMEM((256, 512), F32),
         ),
         in_specs=[hbm, hbm, hbm, vmem, hbm, hbm],
-        out_specs=(hbm, hbm),
+        out_specs=(vmem, vmem),
         scratch_shapes=[
             buf(16, 32, 512), buf(16, 32, 512), buf(8, 512, 1024), buf(32, 4096),
             buf(4, 2, 512, 512), buf(4, 2, 512, 512), buf(4, 2, 512, 512), buf(4, ROWS_A, 512),
@@ -563,8 +548,7 @@
             buf(8, 4, 32, 256), buf(8, 3, 32, 256), buf(8, 3, 2, 32, 256), buf(8, 32, 256),
             buf(16, 2, 2, 4, 32, 256),
             pltpu.VMEM((2, 256, 512), F32), buf(16, 256, 512), buf(2, 2, 4, 256, 512), buf(256, 512),
-            pltpu.VMEM((32, 4096), F32), pltpu.VMEM((256, 512), F32),
-            dma(), dma(), dma(), dma(8), dma(), dma(), dma(2),
+            dma(), dma(), dma(), dma(8), dma(),
             dma(), dma(4, 2), dma(), dma(4), dma(2), dma(2, 2), dma(2), dma(2, 2, 2), dma(), dma(),
             dma(), dma(), dma(), dma(), dma(), dma(2, 2, 4, 2),
             dma(2, 6), dma(8, 6), dma(), dma(2, 2, 4, 2), dma(), dma(2),

time: 119 us -> 116 us (0.975)
  local copies, waits for them, and re-layouts: 3.74 us -> 1.59 us
    unnamed x2, local copies, waits for them, and re-layouts: 3.74 us -> 1.59 us
where the time goes in v4:
time: 116 us; the launch traced here: 115 us
  Pallas kernels  113 us (97%)
  local copies, waits for them, and re-layouts  1.59 us (1%)
    pallas_call x1, Pallas kernels, shards(): pl.pallas_call(kernel, name='distill', out_shape=(pltpu.VMEM((32, 4096),...  113 us

profile of v4, /device:TPU:8, one launch (start us, length us, event | category | flops | bytes accessed | tf_op | source)
XLA Modules:
  0.0 115.4 jit_solution(9962778570687827305)
XLA Ops:
  0.6 113.2 %distill.1 = (f32[32,4096]{1,0:T(8,128)S(1)}, f32[256,512]{1,0:T(8,128)S(1)}) custom-call(bf16[512,512]{1,0:T(8,128)(2,1)} %attn.1, bf16[512,8192]{1,0:T(8,128)(2,1)} %weight.1, bf16[512,512]{1,0:T(8,128)(2,1)} %resid.1, bf16[512]{0:T(512)(128)(2,1)} %gain.1, bf16[512,256]{1,0:T(8,128)(2,1)} %proj.1, bf16[32,4096]{1,0:T(8,128)(2,1)} %student.1), custom_call_target="tpu_custom_call" | custom-call | tf_op jit(solution)/shard_map/distill/pallas_call | solution.py:530
  113.8 0.8 copy.10
  114.6 0.8 copy.11

commit v5 on v4

--- a/solution.py
+++ b/solution.py
@@ -11,7 +11,7 @@
 F32 = jnp.float32
 BF16 = jnp.bfloat16
 BLOCKS = 8
-STEPS = (0, 1, 3, 5, 7, 9, 10, 11)
+STEPS = (0, 0, 2, 4, 6, 8, 8, 9)
 ROWS_A = 160
 HALF_A, HALF_B = ROWS_A // 2, (512 - ROWS_A) // 2
 
@@ -484,20 +484,20 @@
 
     def student_steps(h, carry):
         for par in range(2):
-            for n in reversed(range(len(stages))):
+            for n in (0, 5, 4, 3, 2, 1, 7, 6):
                 m = (par - STEPS[n]) % 2
                 q = h + (par - STEPS[n] - m) // 2
                 pl.when((q >= 0) & (q < BLOCKS))(lambda: stages[n](q, m))
 
             if par == 0:
 
-                @pl.when(h == 0)
+                @pl.when(h == 1)
                 def _():
                     forward(1, 3, 1)
+                    root()
 
                 @pl.when(h == 2)
                 def _():
-                    root()
                     forward(1, 4, 0)
                     forward(1, 4, 1)
 

time: 116 us -> 116 us (level)
  no operation moved by 1% of the time
where the time goes in v5:
time: 116 us; the launch traced here: 115 us
  Pallas kernels  113 us (97%)
  local copies, waits for them, and re-layouts  1.59 us (1%)
    pallas_call x1, Pallas kernels, shards(): pl.pallas_call(kernel, name='distill', out_shape=(pltpu.VMEM((32, 4096),...  113 us

profile of v5, /device:TPU:8, one launch (start us, length us, event | category | flops | bytes accessed | tf_op | source)
XLA Modules:
  0.0 115.1 jit_solution(18274234917612739332)
XLA Ops:
  0.6 112.9 %distill.1 = (f32[32,4096]{1,0:T(8,128)S(1)}, f32[256,512]{1,0:T(8,128)S(1)}) custom-call(bf16[512,512]{1,0:T(8,128)(2,1)} %attn.1, bf16[512,8192]{1,0:T(8,128)(2,1)} %weight.1, bf16[512,512]{1,0:T(8,128)(2,1)} %resid.1, bf16[512]{0:T(512)(128)(2,1)} %gain.1, bf16[512,256]{1,0:T(8,128)(2,1)} %proj.1, bf16[32,4096]{1,0:T(8,128)(2,1)} %student.1), custom_call_target="tpu_custom_call" | custom-call | tf_op jit(solution)/shard_map/distill/pallas_call | solution.py:530
  113.5 0.8 copy.10
  114.3 0.8 copy.11
